TPU v7x, 512 devices: a whole 4x4x16 slice. The times are simulated.
512 devices in a mesh: snap: 64 (over z, y_lo, core), feat: 8 (over y_hi, x).
Axes of the slice: x: 4, y: 4 (y_hi: 2, y_lo: 2; y = y_hi * 2 + y_lo), z: 16, core: 2. Of those that a mesh axis runs over, the one named last changes fastest.
Arguments:
- snapshots: bfloat16 [9728, 8192], P('snap', 'feat'), may hold values from -4.4 to 4.4
- spread: bfloat16 [9728], P('snap'), may hold values from 0.14941406 to 0.5
- start_vectors: float32 [9728, 64], P('snap'), may hold values from -40 to 40
Outputs:
- basis: float32 [9728, 64], P('snap')
All inputs are finite; a program needn't handle non-finite values.
Results may differ from a plain program's by a relative error of at most 0.0013.
Values may be sent and summed in bfloat16 or wider, within the bound.
A program may use at most 64 MiB of HBM per device.

v0:
```python
import jax
import jax.numpy as jnp
from jax import lax
from jax.sharding import PartitionSpec as P

ITERS = 2


def from_behind(block, axis, distance):
    devices = range(lax.axis_size(axis))
    route = [((i - distance) % len(devices), i) for i in devices]
    return lax.ppermute(block, axis, route)


def square_norms(block):
    widened = block.astype(jnp.float32)
    return jnp.sum(widened * widened, axis=1)


def per_device(snapshots, spread, start_vectors):
    snap_count = lax.axis_size("snap")
    half_loop = snap_count // 2
    feat_count = lax.axis_size("feat")
    per_column = half_loop // feat_count
    column = lax.axis_index("feat")
    block_index = lax.axis_index("snap")
    block_rows = snapshots.shape[0]
    features = snapshots.shape[1] * feat_count
    own_norms = square_norms(snapshots)

    def partial_distance(visitor):
        inner = jnp.einsum("sk,tk->st", snapshots, visitor, preferred_element_type=jnp.float32)
        return own_norms[:, None] + square_norms(visitor)[None, :] - 2.0 * inner

    def advance(visitor, unused):
        visitor = from_behind(visitor, "snap", -1)
        return (visitor, partial_distance(visitor))

    unused_last, far_parts = lax.scan(advance, snapshots, None, length=half_loop)
    distances = jnp.concatenate([partial_distance(snapshots)[None], far_parts], axis=0)
    diagonal_sum = lax.psum(distances[0].astype(jnp.bfloat16), "feat").astype(jnp.float32)
    assigned = lax.psum_scatter(distances[1:], "feat", scatter_dimension=0, tiled=True)
    all_widths = (
        lax.all_gather(spread, "snap", axis=0, tiled=True)
        .astype(jnp.float32)
        .reshape(snap_count, block_rows)
    )
    own_widths = spread.astype(jnp.float32)
    offsets = column * per_column + 1 + jnp.arange(per_column, dtype=jnp.int32)
    forward_index = (block_index + offsets) % snap_count
    backward_index = (block_index - offsets + snap_count) % snap_count
    visitor_widths = jnp.take(all_widths, forward_index, axis=0)
    kernel_diagonal = jnp.exp(
        -(diagonal_sum / (own_widths[:, None] * own_widths[None, :])) / features
    ).astype(jnp.bfloat16)
    kernel_forward = jnp.exp(
        -(assigned / (own_widths[None, :, None] * visitor_widths[:, None, :])) / features
    ).astype(jnp.bfloat16)
    moving = kernel_forward
    for bit_number in range(half_loop.bit_length()):
        arrived = from_behind(moving, "snap", 1 << bit_number)
        chosen = offsets >> bit_number & 1 == 1
        moving = jnp.where(chosen[:, None, None], arrived, moving)
    keep_mask = (offsets != half_loop).astype(jnp.bfloat16)
    kernel_backward = moving * keep_mask[:, None, None]
    first_column = (column == 0).astype(jnp.float32)
    local_degree = (
        first_column * jnp.sum(kernel_diagonal.astype(jnp.float32), axis=1)
        + jnp.sum(kernel_forward.astype(jnp.float32), axis=(0, 2))
        + jnp.sum(kernel_backward.astype(jnp.float32), axis=(0, 1))
    )
    degree = lax.psum(local_degree, "feat")
    scale = 1.0 / jnp.sqrt(degree)
    total_rows = block_rows * snap_count
    vectors = start_vectors
    for iteration in range(ITERS):
        weighted = (scale[:, None] * vectors).astype(jnp.bfloat16)
        every_row = lax.all_gather(weighted, "snap", axis=0, tiled=True).reshape(
            snap_count, block_rows, weighted.shape[1]
        )
        forward_rows = jnp.take(every_row, forward_index, axis=0)
        backward_rows = jnp.take(every_row, backward_index, axis=0)
        partial_value = (
            jnp.einsum(
                "qst,qtc->sc", kernel_forward, forward_rows, preferred_element_type=jnp.float32
            )
            + jnp.einsum(
                "qts,qtc->sc", kernel_backward, backward_rows, preferred_element_type=jnp.float32
            )
            + first_column * jnp.dot(kernel_diagonal, weighted, preferred_element_type=jnp.float32)
        )
        image = lax.psum(partial_value, "feat")
        mixed = 0.5 * (vectors + scale[:, None] * image)
        local_gram = jnp.dot(mixed.T, mixed, precision=lax.Precision.HIGHEST)
        gram_matrix = lax.psum(local_gram, "snap") / total_rows
        lower_factor = jnp.linalg.cholesky(gram_matrix)
        vectors = jax.scipy.linalg.solve_triangular(lower_factor, mixed.T, lower=True).T
    return vectors


def solution(mesh):
    return jax.shard_map(
        per_device,
        mesh=mesh,
        in_specs=(P("snap", "feat"), P("snap"), P("snap", None)),
        out_specs=P("snap", None),
        check_vma=False,
    )
```

profile of v0, /device:TPU:1, one launch (start us, length us, event | category | flops | bytes accessed | tf_op | source)
XLA Modules:
  0.0 1553.2 jit_solution(18367044468891227493)
XLA Ops:
  8.6 396.3 %while.12 = (s32[]{:T(128)}, bf16[152,1024]{1,0:T(8,128)(2,1)S(1)}, f32[32,152,152]{2,1,0:T(8,128)}, f32[152]{0:T(256)S(1)}, bf16[152,1024]{1,0:T(8,128)(2,1)}, /*index=5*/s32[]{:T(128)}) while((s32[]{:T(128)}, bf16[152,1024]{1,0:T(8,128)(2,1)S(1)}, f32[32,152,152]{2,1,0:T(8,128)}, f32[152]{0:T(256)S(1)}, bf16[152,1024]{1,0:T(8,128)(2,1)}, ...), condition=%wide.region_5.6_spmd, body=%wide.region_3.0_spmd.sunk | while | flops 47853096 | bytes 2959257 | solution.py:39
  8.6 8.8 collective-permute-start
  20.7 9.7 collective-permute-start
  33.6 9.1 collective-permute-start
  46.0 9.1 collective-permute-start
  58.4 9.1 collective-permute-start
  70.7 9.1 collective-permute-start
  83.1 9.1 collective-permute-start
  95.5 9.1 collective-permute-start
  107.9 9.1 collective-permute-start
  120.2 9.1 collective-permute-start
  132.6 9.1 collective-permute-start
  145.0 9.1 collective-permute-start
  157.4 9.1 collective-permute-start
  169.7 9.1 collective-permute-start
  182.1 9.1 collective-permute-start
  194.5 9.1 collective-permute-start
  206.9 9.1 collective-permute-start
  219.3 9.1 collective-permute-start
  231.6 9.1 collective-permute-start
  244.0 9.1 collective-permute-start
  256.4 9.1 collective-permute-start
  268.8 9.1 collective-permute-start
  281.1 9.1 collective-permute-start
  293.5 9.1 collective-permute-start
  305.9 9.1 collective-permute-start
  318.3 9.1 collective-permute-start
  330.6 9.1 collective-permute-start
  343.0 9.1 collective-permute-start
  355.4 9.1 collective-permute-start
  367.8 9.1 collective-permute-start
  380.1 9.1 collective-permute-start
  392.5 9.1 collective-permute-start
  407.2 215.2 %all-reduce = bf16[9728]{0:T(1024)(128)(2,1)S(1)} all-reduce(bf16[9728]{0:T(1024)(128)(2,1)S(1)} %dynamic-update-slice.2), channel_id=1, replica_groups=mesh['snap'=64,'feat'=8] {'snap'}, use_global_device_ids=true, to_apply=%add | all-reduce | flops 9728 | bytes 38912
  634.2 10.4 collective-permute-done.2
  646.7 6.9 collective-permute-done.3
  655.9 11.0 collective-permute-done.4
  669.0 36.8 %psum.42 = bf16[152,152]{1,0:T(8,128)(2,1)S(1)} all-reduce(bf16[152,152]{1,0:T(8,128)(2,1)S(1)} %fusion.1), channel_id=1, replica_groups=mesh['snap'=64,'feat'=8] {'feat'}, use_global_device_ids=true, to_apply=%region_1.2 | all-reduce | flops 23104 | bytes 92416 | tf_op jit(solution)/shard_map/psum | solution.py:41
  705.8 10.6 collective-permute-start.6
  716.7 14.7 collective-permute-done.6
  731.6 15.7 %psum.43 = f32[152]{0:T(256)S(1)} all-reduce(f32[152]{0:T(256)S(1)} %add_add_fusion), channel_id=1, replica_groups=mesh['snap'=64,'feat'=8] {'feat'}, use_global_device_ids=true, to_apply=%region_9.10 | all-reduce | flops 152 | bytes 1216 | tf_op jit(solution)/shard_map/psum | solution.py:72
  748.1 152.6 %all-gather.5.cloned.1.call-done = bf16[64,152,64]{1,2,0:T(8,128)(2,1)} async-done(((bf16[1,152,64]{1,2,0:T(8,128)(2,1)}), bf16[64,152,64]{1,2,0:T(8,128)(2,1)}) %all-gather.5.cloned.1.call-update) | async-done | bytes 1245200 | tf_op jit(solution)/shard_map/all_gather | solution.py:78
  905.7 34.6 %psum.44 = f32[152,64]{0,1:T(8,128)S(1)} all-reduce(f32[152,64]{0,1:T(8,128)S(1)} %fusion.3), channel_id=1, replica_groups=mesh['snap'=64,'feat'=8] {'feat'}, use_global_device_ids=true, to_apply=%region_10.12 | all-reduce | flops 9728 | bytes 77824 | tf_op jit(solution)/shard_map/psum | solution.py:92
  940.4 210.6 %psum.45 = f32[64,64]{0,1:T(8,128)S(1)} all-reduce(f32[64,64]{0,1:T(8,128)S(1)} %fusion.28), channel_id=1, replica_groups=mesh['snap'=64,'feat'=8] {'snap'}, use_global_device_ids=true, to_apply=%region_11.13 | all-reduce | flops 4096 | bytes 32768 | tf_op jit(solution)/shard_map/psum | solution.py:95
  1151.1 5.8 cholesky.44
  1164.1 119.1 %all-gather.7.cloned.1.call-done = bf16[64,152,64]{1,2,0:T(8,128)(2,1)} async-done(((bf16[1,152,64]{1,2,0:T(8,128)(2,1)}), bf16[64,152,64]{1,2,0:T(8,128)(2,1)}) %all-gather.7.cloned.1.call-update) | async-done | bytes 1245200 | tf_op jit(solution)/shard_map/all_gather | solution.py:78
  1288.3 34.6 %psum.46 = f32[152,64]{0,1:T(8,128)S(1)} all-reduce(f32[152,64]{0,1:T(8,128)S(1)} %fusion.2), channel_id=1, replica_groups=mesh['snap'=64,'feat'=8] {'feat'}, use_global_device_ids=true, to_apply=%region_14.18 | all-reduce | flops 9728 | bytes 77824 | tf_op jit(solution)/shard_map/psum | solution.py:92
  1323.0 210.6 %psum.47 = f32[64,64]{0,1:T(8,128)S(1)} all-reduce(f32[64,64]{0,1:T(8,128)S(1)} %fusion.29), channel_id=1, replica_groups=mesh['snap'=64,'feat'=8] {'snap'}, use_global_device_ids=true, to_apply=%region_15.19 | all-reduce | flops 4096 | bytes 32768 | tf_op jit(solution)/shard_map/psum | solution.py:95
  (212 shorter events, 158.2 us)
Async XLA Ops:
  6.5 616.7 %reduce-scatter.2.cloned.1.call-start = ((), (), s32[]{:S(2)}) async-start(), calls=%async_computation.1 | async-start | bytes 5603328 | tf_op jit(solution)/shard_map/reduce_scatter | solution.py:42
  8.6 396.4 %copy-start.2 = (bf16[152]{0:T(256)(128)(2,1)S(1)}, bf16[152]{0:T(256)(128)(2,1)}, u32[]{:S(2)}) copy-start(bf16[152]{0:T(256)(128)(2,1)} %param.11) | copy-start | bytes 916
  8.6 10.0 collective-permute-start
  20.7 10.9 collective-permute-start
  33.6 10.3 collective-permute-start
  46.0 10.3 collective-permute-start
  58.4 10.3 collective-permute-start
  70.7 10.3 collective-permute-start
  83.1 10.3 collective-permute-start
  95.5 10.3 collective-permute-start
  107.9 10.3 collective-permute-start
  120.2 10.3 collective-permute-start
  132.6 10.3 collective-permute-start
  145.0 10.3 collective-permute-start
  157.4 10.3 collective-permute-start
  169.7 10.3 collective-permute-start
  182.1 10.3 collective-permute-start
  194.5 10.3 collective-permute-start
  206.9 10.3 collective-permute-start
  219.3 10.3 collective-permute-start
  231.6 10.3 collective-permute-start
  244.0 10.3 collective-permute-start
  256.4 10.3 collective-permute-start
  268.8 10.3 collective-permute-start
  281.1 10.3 collective-permute-start
  293.5 10.3 collective-permute-start
  305.9 10.3 collective-permute-start
  318.3 10.3 collective-permute-start
  330.6 10.3 collective-permute-start
  343.0 10.3 collective-permute-start
  355.4 10.3 collective-permute-start
  367.8 10.3 collective-permute-start
  380.1 10.3 collective-permute-start
  392.5 10.3 collective-permute-start
  404.9 250.7 %copy-start = (bf16[152,1024]{1,0:T(8,128)(2,1)S(1)}, bf16[152,1024]{1,0:T(8,128)(2,1)}, u32[]{:S(2)}) copy-start(bf16[152,1024]{1,0:T(8,128)(2,1)} %get-tuple-element.113) | copy-start | bytes 933892
  404.9 342.4 %copy-start.1 = (f32[152,64]{0,1:T(8,128)S(1)}, f32[152,64]{0,1:T(8,128)}, u32[]{:S(2)}) copy-start(f32[152,64]{0,1:T(8,128)} %param.12) | copy-start | bytes 116740
  404.9 495.7 %all-gather.5.cloned.1.call-start = ((), (), s32[]{:S(2)}) async-start(), calls=%async_computation.2 | async-start | bytes 2129920 | tf_op jit(solution)/shard_map/all_gather | solution.py:78
  624.7 7.4 collective-permute-start.1
  632.3 12.4 collective-permute-start.2
  644.8 8.9 collective-permute-start.3
  653.7 13.2 collective-permute-start.4
  667.0 38.7 %collective-permute-start.5 = (bf16[4,152,152]{2,1,0:T(8,128)(2,1)S(1)}, bf16[4,152,152]{2,1,0:T(8,128)(2,1)S(1)}, u32[]{:S(2)}, u32[]{:S(2)}) collective-permute-start(bf16[4,152,152]{2,1,0:T(8,128)(2,1)S(1)} %broadcast_select_fusion.3), channel_id=1, source_target_pairs={{384,0},{392,8},{400,16},{408,24},{416,32},{424,40},{432,48},{440,... | collective-permute-start | bytes 554504 | tf_op jit(solution)/shard_map/ppermute | solution.py:12
  705.8 25.5 %collective-permute-start.6 = (bf16[4,152,152]{2,1,0:T(8,128)(2,1)S(1)}, bf16[4,152,152]{2,1,0:T(8,128)(2,1)S(1)}, u32[]{:S(2)}, u32[]{:S(2)}) collective-permute-start(bf16[4,152,152]{2,1,0:T(8,128)(2,1)S(1)} %broadcast_select_fusion.4), channel_id=1, source_target_pairs={{256,0},{264,8},{272,16},{280,24},{288,32},{296,40},{304,48},{312,... | collective-permute-start | bytes 554504 | tf_op jit(solution)/shard_map/ppermute | solution.py:12
  748.0 535.3 %all-gather.7.cloned.1.call-start = ((), (), s32[]{:S(2)}) async-start(), calls=%async_computation.3 | async-start | bytes 2129920 | tf_op jit(solution)/shard_map/all_gather | solution.py:78
Sparse Core Ops, SparseCore 0:
  405.0 108.0 reduce-scatter.1
  748.1 152.5 all-gather.4
  1164.2 118.9 all-gather.6
where the time goes:
time: 1560 us; the launch traced here: 1550 us
  blocking collectives  758 us (49%)
  waiting for transfers between devices  357 us (23%)
  starting transfers between devices  313 us (20%)
  matrix products  63.8 us (4%)
  other arithmetic  33.7 us (2%)
    psum x2, blocking collectives, per_device(): gram_matrix = lax.psum(local_gram, 'snap') / total_rows  421 us
    ppermute x38, starting transfers between devices, from_behind(): return lax.ppermute(block, axis, route)  313 us
    all_gather x2, waiting for transfers between devices, per_device(): lax.all_gather(weighted, 'snap', axis=0, tiled=True)  272 us
    unnamed x1, blocking collectives  215 us
    ppermute x38, waiting for transfers between devices, from_behind(): return lax.ppermute(block, axis, route)  85.6 us
    psum x2, blocking collectives, per_device(): image = lax.psum(partial_value, 'feat')  69.1 us
    dot_general x33, matrix products, partial_distance(): jnp.einsum('sk,tk->st', snapshots, visitor, preferred_element_type=jnp.fl...  60.8 us
    psum x1, blocking collectives, per_device(): lax.psum(distances[0].astype(jnp.bfloat16), 'feat').astype(jnp.float32)  36.8 us
  transfers between devices with their start and end apart: 41, of which 39 were waited for; matrix products, arithmetic and copies ran while one was open for 0% of the time, Pallas kernels for 0%

commit v1 on v0

v1 whole, which is shorter than its diff:
```python
import functools

import jax
import jax.numpy as jnp
from jax import lax
from jax.experimental import pallas as pl
from jax.experimental.pallas import tpu as pltpu
from jax.sharding import PartitionSpec as P

ITERS = 2
Z = 16
Q = 4
NF = 8
NX = 4
HOPS = 4
ROWS = 152
PAD = 160
WIDE = Q * PAD
NV = 64
FEATURES = 8192
TOTAL = Z * Q * ROWS
F32 = jnp.float32
BF16 = jnp.bfloat16
HIGHEST = lax.Precision.HIGHEST


class Ids:
    def __init__(self):
        self.count = 0

    def take(self, number=1):
        first = self.count
        self.count += number
        return first


def dot_nt(a, b, precision=None):
    return lax.dot_general(
        a, b, (((1,), (1,)), ((), ())), precision=precision, preferred_element_type=F32
    )


def dot_nn(a, b, precision=None):
    return lax.dot_general(
        a, b, (((1,), (0,)), ((), ())), precision=precision, preferred_element_type=F32
    )


def eye(rows, columns):
    row = lax.broadcasted_iota(jnp.int32, (rows, columns), 0)
    column = lax.broadcasted_iota(jnp.int32, (rows, columns), 1)
    return row == column


def column_of(row):
    n = row.shape[1]
    return jnp.sum(jnp.where(eye(n, n), row, 0.0), axis=1, keepdims=True)


def row_norms(block):
    wide = block.astype(F32)
    return jnp.sum(wide * wide, axis=1, keepdims=True)


def inverse_factor(gram):
    n = gram.shape[0]
    both = jnp.concatenate([gram, eye(n, n).astype(F32)], axis=1)
    rows = lax.broadcasted_iota(jnp.int32, (n, 1), 0)
    for j in range(n - 1):
        pivot_row = both[j : j + 1, :]
        factor = both[:, j : j + 1] * (1.0 / pivot_row[:, j : j + 1])
        both = both - jnp.where(rows > j, factor, 0.0) * pivot_row
    diagonal = jnp.sum(jnp.where(eye(n, n), both[:, :n], 0.0), axis=1, keepdims=True)
    return both[:, n:] * lax.rsqrt(diagonal)


def count_ids():
    ids = Ids()
    names = {}
    names["up"] = ids.take(HOPS + 1)
    names["down"] = ids.take(HOPS + 1)
    names["across"] = ids.take(HOPS + 1)
    names["mate"] = ids.take(HOPS + 1)
    names["mate2"] = ids.take(HOPS + 1)
    names["x_send"] = ids.take(9)
    names["x_recv"] = ids.take(9)
    names["y"] = ids.take(2)
    names["gather"] = ids.take((ITERS + 1) * 8)
    names["parts"] = ids.take((ITERS + 1) * 5)
    names["feat"] = ids.take((ITERS + 1) * 8)
    names["gram_q"] = ids.take(ITERS * 4)
    names["gram_z"] = ids.take(ITERS * 2)
    names["gram_f"] = ids.take(ITERS * 8)
    return names, ids.count


NAMES, N_IDS = count_ids()


def kernel(
    x_ref,
    spread_ref,
    start_ref,
    out_ref,
    cbuf,
    rbuf,
    pbuf,
    xbuf,
    ysend,
    yrecv,
    keep,
    kq,
    k0,
    width_src,
    width_c,
    width_r,
    width_0,
    w_src,
    w_c,
    w_r,
    w_0,
    d_src,
    dc_src,
    d_r,
    d_c,
    d_f,
    i_src,
    ic_src,
    i_r,
    i_c,
    i_f,
    g_q,
    g_zsrc,
    g_z,
    g_f,
    send_sem,
    recv_sem,
):
    snap = lax.axis_index("snap")
    f = lax.axis_index("feat")
    z = snap // Q
    q = snap % Q
    x = f % NX
    yh = f // NX
    k = f + 1
    r_off = (k + 1) // 2
    c_off = k // 2
    q_across = (q + 2) % Q
    q_mate = q + 1 - 2 * (q % 2)
    q_both = (q_mate + 2) % Q

    def at(zz, qq, ff):
        return {"snap": ((zz + Z) % Z) * Q + qq, "feat": ff}

    pending = []

    def copy(src, dst, name, send, recv, device, when=None):
        made = pltpu.make_async_remote_copy(
            src_ref=src,
            dst_ref=dst,
            send_sem=send_sem.at[NAMES[name] + send],
            recv_sem=recv_sem.at[NAMES[name if name != "x_send" else "x_recv"] + recv],
            device_id=device,
            device_id_type=pl.DeviceIdType.MESH,
        )
        if when is None:
            made.start()
        else:
            pl.when(when)(made.start)
        pending.append((made, when))

    def arrived(dst, name, recv):
        pltpu.make_async_remote_copy(
            src_ref=dst,
            dst_ref=dst,
            send_sem=send_sem.at[NAMES[name]],
            recv_sem=recv_sem.at[NAMES[name] + recv],
            device_id=at(z, q_mate, f),
            device_id_type=pl.DeviceIdType.MESH,
        ).wait_recv()

    barrier = pltpu.get_barrier_semaphore()
    first = f == 0
    not_first = f != 0

    def greet(device):
        pl.semaphore_signal(
            barrier, inc=1, device_id=device, device_id_type=pl.DeviceIdType.MESH
        )

    greet(at(z + 1, q, f))
    greet(at(z - 1, q, f))
    for i in range(1, Q):
        greet(at(z, (q + i) % Q, f))
    for i in range(1, NF):
        greet(at(z, q, (f + i) % NF))
    for i in range(Q):
        greet(at(z + r_off, i, f))
        greet(at(z - r_off, i, f))
    greet(at(z + 8 + f, q, f))

    @pl.when(not_first)
    def _():
        greet(at(z + c_off, q, f))
        greet(at(z - c_off, q, f))
        greet(at(z + f, q, f))

    cbuf[0, :ROWS, :] = x_ref[...]
    cbuf[0, ROWS:, :] = jnp.zeros((PAD - ROWS, cbuf.shape[2]), BF16)
    lane = lax.broadcasted_iota(jnp.int32, (1, PAD), 1)
    width_src[...] = jnp.broadcast_to(
        jnp.concatenate(
            [spread_ref[...].astype(F32), jnp.ones((1, PAD - ROWS), F32)], axis=1
        ),
        (8, PAD),
    )
    pl.semaphore_wait(barrier, 2 + 3 + 7 + 8 + 1 + 3 * not_first.astype(jnp.int32))

    def spread_out(src, c_dst, r_dst, z_dst, base):
        for i in range(Q):
            copy(src, r_dst.at[q], "gather", base + i, base + q, at(z - r_off, i, f))
        copy(src, c_dst, "gather", base + 4, base + 4, at(z + c_off, q, f), not_first)

        @pl.when(first)
        def _():
            c_dst[...] = src[...]
            z_dst[q] = src[...]

        for i in range(1, Q):
            copy(src, z_dst.at[q], "gather", base + 4 + i, base + 4 + i, at(z, (q + i) % Q, f), first)

    def spread_in(c_dst, r_dst, z_dst, base):
        for i in range(Q):
            arrived(r_dst.at[i], "gather", base + i)
        pl.when(not_first)(lambda: arrived(c_dst, "gather", base + 4))

        @pl.when(first)
        def _():
            for i in range(1, Q):
                arrived(z_dst.at[(q + Q - i) % Q], "gather", base + 4 + i)

    copy(cbuf.at[0], cbuf.at[1], "up", 1, 1, at(z + 1, q, f))
    copy(cbuf.at[0], rbuf.at[1, q], "down", 1, 1, at(z - 1, q, f))
    copy(cbuf.at[0], rbuf.at[0, q], "across", 0, 0, at(z, q_across, f))
    copy(cbuf.at[0], rbuf.at[0, q], "mate", 0, 0, at(z, q_mate, f))
    rbuf[0, q] = cbuf[0]
    spread_out(width_src, width_c, width_r, width_0, 0)

    def rows_arrive(h):
        arrived(rbuf.at[h, q_across], "across", h)
        copy(rbuf.at[h, q_across], rbuf.at[h, q_across], "mate2", h, h, at(z, q_mate, f))

    def tile_parts(h):
        arrived(rbuf.at[h, q_mate], "mate", h)
        arrived(rbuf.at[h, q_both], "mate2", h)
        wide_row = lax.broadcasted_iota(jnp.int32, (PAD, WIDE), 0)
        wide_lane = lax.broadcasted_iota(jnp.int32, (PAD, WIDE), 1)
        picked = jnp.zeros((PAD, WIDE), F32)
        for i in range(Q):
            picked = jnp.where(wide_lane == wide_row + i * PAD, row_norms(rbuf[h, i]), picked)
        r_norms = jnp.sum(picked, axis=0, keepdims=True)
        r_block = rbuf[h].reshape(WIDE, rbuf.shape[3])
        for kk, c in [(0, 0)] if h == 0 else [(2 * h - 1, h - 1), (2 * h, h)]:
            inner = dot_nt(cbuf[c], r_block)
            pbuf[kk] = (row_norms(cbuf[c]) + r_norms - 2.0 * inner).astype(BF16)
            owner, slot = (0, 2) if kk == 0 else ((kk - 1) % NX, (kk - 1) // NX)
            source = (x - owner + NX - 1) % NX
            copy(
                pbuf.at[kk],
                xbuf.at[slot, source % 3],
                "x_send",
                kk,
                slot * 3 + source % 3,
                at(z, q, yh * NX + owner),
                x != owner,
            )

    def sum_x(kk):
        owner, slot = (0, 2) if kk == 0 else ((kk - 1) % NX, (kk - 1) // NX)
        last = 0 if kk == 0 else slot
        kind = 1 if kk == 0 else 0

        @pl.when(x == owner)
        def _():
            for i in range(3):
                arrived(xbuf.at[slot, i], "x_recv", slot * 3 + i)
            total = pbuf[kk].astype(F32)
            for i in range(3):
                total = total + xbuf[slot, i].astype(F32)

            @pl.when(yh == last)
            def _():
                keep[kind] = total

            @pl.when(yh != last)
            def _():
                ysend[kind] = total.astype(BF16)

        copy(
            ysend.at[kind],
            yrecv.at[kind],
            "y",
            kind,
            kind,
            at(z, q, (f + NX) % NF),
            (x == owner) & (yh != last),
        )

    for step in range(HOPS + 3):
        if 1 <= step <= HOPS:
            h = step
            arrived(rbuf.at[h, q], "down", h)
            if h < HOPS:
                copy(rbuf.at[h, q], rbuf.at[h + 1, q], "down", h + 1, h + 1, at(z - 1, q, f))
            copy(rbuf.at[h, q], rbuf.at[h, q], "across", h, h, at(z, q_across, f))
            copy(rbuf.at[h, q], rbuf.at[h, q], "mate", h, h, at(z, q_mate, f))
            arrived(cbuf.at[h], "up", h)
            if h < HOPS:
                copy(cbuf.at[h], cbuf.at[h + 1], "up", h + 1, h + 1, at(z + 1, q, f))
        if 1 <= step <= HOPS + 1:
            rows_arrive(step - 1)
            tile_parts(step - 1)
        if step >= 2:
            h = step - 2
            for kk in [0] if h == 0 else [2 * h - 1, 2 * h]:
                sum_x(kk)

    spread_in(width_c, width_r, width_0, 0)

    def kernel_blocks(total, c_width, r_width, dst):
        c_column = column_of(c_width)
        row = lax.broadcasted_iota(jnp.int32, (PAD, PAD), 0)
        column = lax.broadcasted_iota(jnp.int32, (PAD, PAD), 1)
        inside = (row < ROWS) & (column < ROWS)
        for i in range(Q):
            distance = total[:, i * PAD : (i + 1) * PAD]
            exponent = -(distance / (c_column * r_width[i, :1, :])) / FEATURES
            dst[i] = jnp.where(inside, jnp.exp(exponent), 0.0).astype(BF16)

    arrived(yrecv.at[0], "y", 0)
    kernel_blocks(keep[0] + yrecv[0].astype(F32), width_c[:1, :], width_r, kq)

    @pl.when(first)
    def _():
        arrived(yrecv.at[1], "y", 1)
        kernel_blocks(keep[1] + yrecv[1].astype(F32), width_src[:1, :], width_0, k0)

    def product(index, height, c_rows, r_rows, z_rows, src, c_src, got_r, got_c, got_f):
        for i in range(Q):
            src[i] = dot_nn(c_rows, kq[i])[:height]
        part = dot_nt(r_rows(0), kq[0])
        for i in range(1, Q):
            part = part + dot_nt(r_rows(i), kq[i])
        part = part[:height]

        @pl.when(not_first)
        def _():
            c_src[...] = part

        @pl.when(first)
        def _():
            own = part
            for i in range(Q):
                own = own + dot_nt(z_rows(i), k0[i])[:height]
            got_c[...] = own

        @pl.when(f == NF - 1)
        def _():
            got_c[...] = jnp.zeros_like(got_c)

        base = index * 5
        middle = not_first & (f != NF - 1)
        for i in range(Q):
            copy(src.at[i], got_r.at[q], "parts", base + i, base + q, at(z + r_off, i, f))
        copy(c_src, got_c, "parts", base + 4, base + 4, at(z - c_off, q, f), middle)
        for i in range(Q):
            arrived(got_r.at[i], "parts", base + i)
        pl.when(middle)(lambda: arrived(got_c, "parts", base + 4))
        total = got_c[...]
        for i in range(Q):
            total = total + got_r[i]
        return sum_feat(total, got_f, "feat", index * 8)

    def sum_feat(total, got_f, name, base):
        got_f[f] = total
        for i in range(1, NF):
            copy(got_f.at[f], got_f.at[f], name, base + i, base + i, at(z, q, (f + i) % NF))
        for i in range(1, NF):
            arrived(got_f.at[(f + NF - i) % NF], name, base + i)
        total = got_f[0]
        for i in range(1, NF):
            total = total + got_f[i]
        return total

    ones = jnp.ones((16, PAD), BF16)
    degree = product(
        0, 8, ones, lambda i: ones, lambda i: ones, d_src, dc_src, d_r, d_c, d_f
    )[:1]
    scale = jnp.where(lane < ROWS, 1.0 / jnp.sqrt(jnp.where(lane < ROWS, degree, 1.0)), 0.0)

    start = jnp.concatenate(
        [start_ref[...], jnp.zeros((PAD - ROWS, NV), F32)], axis=0
    )
    vectors = dot_nt(eye(NV, NV).astype(F32), start, HIGHEST)
    for it in range(ITERS):
        w_src[it] = (scale * vectors).astype(BF16)
        spread_out(w_src.at[it], w_c.at[it], w_r.at[it], w_0.at[it], 8 * (it + 1))
        spread_in(w_c.at[it], w_r.at[it], w_0.at[it], 8 * (it + 1))
        image = product(
            it + 1,
            NV,
            w_c[it],
            lambda i, it=it: w_r[it, i],
            lambda i, it=it: w_0[it, i],
            i_src.at[it],
            ic_src.at[it],
            i_r.at[it],
            i_c.at[it],
            i_f.at[it],
        )
        mixed = 0.5 * (vectors + scale * image)
        g_q[it, q] = dot_nt(mixed, mixed, HIGHEST)
        for i in range(1, Q):
            copy(g_q.at[it, q], g_q.at[it, q], "gram_q", 4 * it + i, 4 * it + i, at(z, (q + i) % Q, f))
        for i in range(1, Q):
            arrived(g_q.at[it, (q + Q - i) % Q], "gram_q", 4 * it + i)
        here = g_q[it, 0]
        for i in range(1, Q):
            here = here + g_q[it, i]
        g_zsrc[it] = here

        @pl.when(first)
        def _():
            g_z[it, 0] = here

        copy(g_zsrc.at[it], g_z.at[it, 0], "gram_z", 2 * it, 2 * it, at(z - f, q, f), not_first)
        copy(g_zsrc.at[it], g_z.at[it, 1], "gram_z", 2 * it + 1, 2 * it + 1, at(z + 8 - f, q, f))
        pl.when(not_first)(lambda it=it: arrived(g_z.at[it, 0], "gram_z", 2 * it))
        arrived(g_z.at[it, 1], "gram_z", 2 * it + 1)
        gram = sum_feat(g_z[it, 0] + g_z[it, 1], g_f.at[it], "gram_f", 8 * it)
        inverse = inverse_factor(gram / TOTAL)
        vectors = dot_nn(inverse, mixed, HIGHEST)

    out_ref[...] = dot_nt(eye(PAD, PAD).astype(F32), vectors, HIGHEST)[:ROWS]
    for made, when in pending:
        if when is None:
            made.wait_send()
        else:
            pl.when(when)(made.wait_send)


def per_device(snapshots, spread, start_vectors):
    depth = snapshots.shape[1]
    vmem = pltpu.VMEM
    shapes = [
        vmem((HOPS + 1, PAD, depth), BF16),
        vmem((HOPS + 1, Q, PAD, depth), BF16),
        vmem((9, PAD, WIDE), BF16),
        vmem((3, 3, PAD, WIDE), BF16),
        vmem((2, PAD, WIDE), BF16),
        vmem((2, PAD, WIDE), BF16),
        vmem((2, PAD, WIDE), F32),
        vmem((Q, PAD, PAD), BF16),
        vmem((Q, PAD, PAD), BF16),
        vmem((8, PAD), F32),
        vmem((8, PAD), F32),
        vmem((Q, 8, PAD), F32),
        vmem((Q, 8, PAD), F32),
        vmem((ITERS, NV, PAD), BF16),
        vmem((ITERS, NV, PAD), BF16),
        vmem((ITERS, Q, NV, PAD), BF16),
        vmem((ITERS, Q, NV, PAD), BF16),
        vmem((Q, 8, PAD), F32),
        vmem((8, PAD), F32),
        vmem((Q, 8, PAD), F32),
        vmem((8, PAD), F32),
        vmem((NF, 8, PAD), F32),
        vmem((ITERS, Q, NV, PAD), F32),
        vmem((ITERS, NV, PAD), F32),
        vmem((ITERS, Q, NV, PAD), F32),
        vmem((ITERS, NV, PAD), F32),
        vmem((ITERS, NF, NV, PAD), F32),
        vmem((ITERS, Q, NV, NV), F32),
        vmem((ITERS, NV, NV), F32),
        vmem((ITERS, 2, NV, NV), F32),
        vmem((ITERS, NF, NV, NV), F32),
        pltpu.SemaphoreType.DMA((N_IDS,)),
        pltpu.SemaphoreType.DMA((N_IDS,)),
    ]
    return pl.pallas_call(
        kernel,
        out_shape=jax.ShapeDtypeStruct(start_vectors.shape, F32),
        in_specs=[pl.BlockSpec(memory_space=pltpu.VMEM)] * 3,
        out_specs=pl.BlockSpec(memory_space=pltpu.VMEM),
        scratch_shapes=shapes,
        compiler_params=pltpu.CompilerParams(
            collective_id=0, has_side_effects=True, vmem_limit_bytes=40 * 1024 * 1024
        ),
        cost_estimate=pl.CostEstimate(
            flops=4_000_000_000, bytes_accessed=400_000, transcendentals=200_000
        ),
        name="subspace",
    )(snapshots, spread.reshape(1, -1), start_vectors)


def solution(mesh):
    return jax.shard_map(
        per_device,
        mesh=mesh,
        in_specs=(P("snap", "feat"), P("snap"), P("snap", None)),
        out_specs=P("snap", None),
        check_vma=False,
    )
```

time: 1560 us -> 218 us (0.14)
  blocking collectives: 758 us -> 0 us
  waiting for transfers between devices: 357 us -> 0 us
  starting transfers between devices: 313 us -> 0 us
  Pallas kernels: 0 us -> 213 us
  matrix products: 63.8 us -> 0 us
  other arithmetic: 33.7 us -> 0 us
    psum x6 -> x0, blocking collectives: 543 us -> none  [the longest x2 421 us: per_device(): gram_matrix = lax.psum(local_gram, 'snap') / total_rows]
    ppermute x38 -> x0, starting transfers between devices: 313 us -> none  [from_behind(): return lax.ppermute(block, axis, route)]
    all_gather x2 -> x0, waiting for transfers between devices: 272 us -> none  [per_device(): lax.all_gather(weighted, 'snap', axis=0, tiled=True)]
    unnamed x1 -> x0, blocking collectives: 215 us -> none
    pallas_call x0 -> x1, Pallas kernels: none -> 213 us  [per_device(): pl.pallas_call(kernel, out_shape=jax.ShapeDtypeStruct(start_vectors.shape...]
    ppermute x38 -> x0, waiting for transfers between devices: 85.6 us -> none  [from_behind(): return lax.ppermute(block, axis, route)]
    dot_general x41 -> x0, matrix products: 62.6 us -> none  [the longest x33 60.8 us: partial_distance(): jnp.einsum('sk,tk->st', snapshots, visitor, preferred_element_type=jnp.fl...]
    another operation x10 -> x0, other arithmetic: 24.1 us -> none  [the longest x6 13 us: per_device(): lower_factor = jnp.linalg.cholesky(gram_matrix)]
  transfers between devices with their start and end apart: 41 -> 0, of which waited for: 39 -> 0; matrix products, arithmetic and copies ran while one was open for 0% -> 0% of each run, Pallas kernels for 0% -> 0%
where the time goes in v1:
time: 218 us; the launch traced here: 216 us
  Pallas kernels  213 us (98%)
  local copies, waits for them, and re-layouts  3.27 us (2%)
    pallas_call x1, Pallas kernels, per_device(): pl.pallas_call(kernel, out_shape=jax.ShapeDtypeStruct(start_vectors.shape...  213 us

profile of v1, /device:TPU:1, one launch (start us, length us, event | category | flops | bytes accessed | tf_op | source)
XLA Modules:
  0.0 216.1 jit_solution(1258770422487138229)
XLA Ops:
  0.0 0.7 reshape.3.spread_ref
  0.7 0.9 copy.4.start_ref
  1.6 0.0 copy-start
  1.6 1.0 copy-done
  2.6 212.8 %subspace.1 = f32[152,64]{1,0:T(8,128)S(1)} custom-call(bf16[152,1024]{1,0:T(8,128)(2,1)S(1)} %copy-done, bf16[1,152]{1,0:T(2,128)(2,1)S(1)} %reshape.3.spread_ref, f32[152,64]{1,0:T(8,128)S(1)} %copy.4.start_ref), custom_call_target="tpu_custom_call" | custom-call | flops 4000000000 | bytes 400000 | tf_op jit(solution)/shard_map/subspace/pallas_call | solution.py:490
  215.4 0.7 copy.5
Async XLA Ops:
  1.6 1.0 copy-start

commit v2 on v1

v2 whole, which is shorter than its diff:
```python
import jax
import jax.numpy as jnp
from jax import lax
from jax.experimental import pallas as pl
from jax.experimental.pallas import tpu as pltpu
from jax.sharding import PartitionSpec as P

Z = 16
Q = 4
NF = 8
NX = 4
HOPS = 4
HALVES = 2
ROWS = 152
PAD = 160
WIDE = 4 * PAD
NV = 64
FEATURES = 8192
TOTAL = Z * Q * ROWS
F32 = jnp.float32
BF16 = jnp.bfloat16
HIGHEST = lax.Precision.HIGHEST
R_OFF = (0, 1, 1, 2, 2, 3, 3, 3, 4)
C_OFF = (0, 0, 1, 1, 2, 2, 3, 4, 4)


def dot_nt(a, b, precision=None):
    return lax.dot_general(
        a, b, (((1,), (1,)), ((), ())), precision=precision, preferred_element_type=F32
    )


def dot_nn(a, b, precision=None):
    return lax.dot_general(
        a, b, (((1,), (0,)), ((), ())), precision=precision, preferred_element_type=F32
    )


def eye(n):
    row = lax.broadcasted_iota(jnp.int32, (n, n), 0)
    column = lax.broadcasted_iota(jnp.int32, (n, n), 1)
    return row == column


def column_of(row):
    return jnp.sum(jnp.where(eye(row.shape[1]), row, 0.0), axis=1, keepdims=True)


def row_of(column):
    return jnp.sum(jnp.where(eye(column.shape[0]), column, 0.0), axis=0, keepdims=True)


def inverse_factor(gram):
    n = gram.shape[0]
    both = jnp.concatenate([gram, eye(n).astype(F32)], axis=1)
    rows = lax.broadcasted_iota(jnp.int32, (n, 1), 0)
    for j in range(n - 1):
        pivot_row = both[j : j + 1, :]
        factor = both[:, j : j + 1] * (1.0 / pivot_row[:, j : j + 1])
        both = both - jnp.where(rows > j, factor, 0.0) * pivot_row
    diagonal = jnp.sum(jnp.where(eye(n), both[:, :n], 0.0), axis=1, keepdims=True)
    return both[:, n:] * lax.rsqrt(diagonal)


def count_ids():
    sizes = {
        "up": (HOPS + 1) * HALVES,
        "down": (HOPS + 1) * HALVES,
        "across": (HOPS + 1) * HALVES,
        "mate": (HOPS + 1) * HALVES,
        "x": 9,
        "y": 2,
        "gather": 3 * 5,
        "parts": 3 * 4,
        "feat": 3 * 8,
        "gram_q": 2 * 4,
        "gram_z": 2 * 2,
        "gram_f": 2 * 8,
    }
    names, count = {}, 0
    for name, size in sizes.items():
        names[name] = count
        count += size
    return names, count


NAMES, N_IDS = count_ids()


def kernel(
    x_ref,
    spread_ref,
    start_ref,
    out_ref,
    cbuf,
    rbuf,
    pbuf,
    xbuf,
    ysend,
    yrecv,
    keep,
    kq,
    k0,
    width_src,
    width_c,
    width_r,
    width_0,
    w_src,
    w_c,
    w_r,
    w_0,
    d_rsrc,
    d_csrc,
    d_r,
    d_c,
    d_f,
    i_rsrc,
    i_csrc,
    i_r,
    i_c,
    i_f,
    g_q,
    g_zsrc,
    g_z,
    g_f,
    send_sem,
    recv_sem,
):
    snap = lax.axis_index("snap")
    f = lax.axis_index("feat")
    z = snap // Q
    q = snap % Q
    y = q // 2
    c = q % 2
    x = f % NX
    yh = f // NX
    k = f + 1
    is_7 = (k == 7).astype(jnp.int32)
    r_off = (k + 1) // 2 - is_7
    c_off = k // 2 + is_7
    first = f == 0
    not_first = f != 0
    has_c = not_first & (f != NF - 1)
    half_depth = cbuf.shape[4]

    def at(zz, yy, cc, ff):
        return {"snap": ((zz + Z) % Z) * Q + yy * 2 + cc, "feat": ff}

    across = at(z, 1 - y, c, f)
    mate = at(z, y, 1 - c, f)
    pending = []

    def copy(src, dst, name, send, recv, device, when=None):
        made = pltpu.make_async_remote_copy(
            src_ref=src,
            dst_ref=dst,
            send_sem=send_sem.at[NAMES[name] + send],
            recv_sem=recv_sem.at[NAMES[name] + recv],
            device_id=device,
            device_id_type=pl.DeviceIdType.MESH,
        )
        if when is None:
            made.start()
        else:
            pl.when(when)(made.start)
        pending.append((made, when))

    def arrived(dst, name, recv):
        pltpu.make_async_remote_copy(
            src_ref=dst,
            dst_ref=dst,
            send_sem=send_sem.at[NAMES[name]],
            recv_sem=recv_sem.at[NAMES[name] + recv],
            device_id=mate,
            device_id_type=pl.DeviceIdType.MESH,
        ).wait_recv()

    barrier = pltpu.get_barrier_semaphore()
    near = [at(z + 1, y, c, f), at(z - 1, y, c, f), across, mate]
    near += [at(z, y, c, yh * NX + (x + i) % NX) for i in range(1, NX)]
    near += [at(z, y, c, (f + NX) % NF)]
    for device in near:
        pl.semaphore_signal(
            barrier, inc=1, device_id=device, device_id_type=pl.DeviceIdType.MESH
        )
    for half in range(HALVES):
        part = x_ref[:, half * half_depth : (half + 1) * half_depth]
        rest = jnp.zeros((PAD - ROWS, half_depth), BF16)
        cbuf[0, c, half, :ROWS, :] = part
        cbuf[0, c, half, ROWS:, :] = rest
        rbuf[0, y, half, :ROWS, :] = part
        rbuf[0, y, half, ROWS:, :] = rest
    lane = lax.broadcasted_iota(jnp.int32, (1, PAD), 1)
    width_src[...] = jnp.broadcast_to(
        jnp.concatenate(
            [spread_ref[...].astype(F32), jnp.ones((1, PAD - ROWS), F32)], axis=1
        ),
        (8, PAD),
    )
    pl.semaphore_wait(barrier, len(near))

    def send_down(h, half):
        src = rbuf.at[h, y, half]
        if h < HOPS:
            number = (h + 1) * HALVES + half
            copy(src, rbuf.at[h + 1, y, half], "down", number, number, at(z - 1, y, c, f))
        number = h * HALVES + half
        copy(src, rbuf.at[h, y, half], "across", number, number, across)

    def send_up(h, half):
        src = cbuf.at[h, c, half]
        if h < HOPS:
            number = (h + 1) * HALVES + half
            copy(src, cbuf.at[h + 1, c, half], "up", number, number, at(z + 1, y, c, f))
        number = h * HALVES + half
        copy(src, cbuf.at[h, c, half], "mate", number, number, mate)

    def travel(h, halves=range(HALVES)):
        for half in halves:
            number = h * HALVES + half
            if h > 0:
                arrived(rbuf.at[h, y, half], "down", number)
            send_down(h, half)
            if h > 0:
                arrived(cbuf.at[h, c, half], "up", number)
            send_up(h, half)

    def norms(ref, h, i):
        total = jnp.zeros((PAD, 1), F32)
        for half in range(HALVES):
            wide = ref[h, i, half].astype(F32)
            total = total + jnp.sum(wide * wide, axis=1, keepdims=True)
        return total

    def owner_of(kk):
        return (0, 0, 2) if kk == 0 else ((kk - 1) % NX, (kk - 1) // NX, (kk - 1) // NX)

    def make_tile(kk):
        r, h = R_OFF[kk], C_OFF[kk]
        c_norms = [norms(cbuf, h, j) for j in range(2)]
        r_norms = [row_of(norms(rbuf, r, i)) for i in range(2)]
        blocks = []
        for j in range(2):
            for i in range(2):
                inner = dot_nt(cbuf[h, j, 0], rbuf[r, i, 0])
                for half in range(1, HALVES):
                    inner = inner + dot_nt(cbuf[h, j, half], rbuf[r, i, half])
                blocks.append(c_norms[j] + r_norms[i] - 2.0 * inner)
        pbuf[kk] = jnp.concatenate(blocks, axis=1).astype(BF16)
        owner, _, slot = owner_of(kk)
        source = (x - owner + NX - 1) % NX % 3
        copy(
            pbuf.at[kk],
            xbuf.at[slot, source],
            "x",
            kk,
            slot * 3 + source,
            at(z, y, c, yh * NX + owner),
            x != owner,
        )

    def sum_x(kk):
        owner, last, slot = owner_of(kk)
        kind = 1 if kk == 0 else 0

        @pl.when(x == owner)
        def _():
            for i in range(3):
                arrived(xbuf.at[slot, i], "x", slot * 3 + i)
            total = pbuf[kk].astype(F32)
            for i in range(3):
                total = total + xbuf[slot, i].astype(F32)

            @pl.when(yh == last)
            def _():
                keep[kind] = total

            @pl.when(yh != last)
            def _():
                ysend[kind] = total.astype(BF16)

        copy(
            ysend.at[kind],
            yrecv.at[kind],
            "y",
            kind,
            kind,
            at(z, y, c, (f + NX) % NF),
            (x == owner) & (yh != last),
        )

    def rows_in(h):
        for half in range(HALVES):
            arrived(rbuf.at[h, 1 - y, half], "across", h * HALVES + half)

    def columns_in(h):
        for half in range(HALVES):
            arrived(cbuf.at[h, 1 - c, half], "mate", h * HALVES + half)

    def spread_out(src, c_dst, r_dst, z_dst, base):
        for i in range(2):
            copy(src, r_dst.at[y], "gather", base + i, base + y, at(z - r_off, i, c, f))
        for i in range(2):
            number = base + 2 + i
            copy(src, c_dst.at[c], "gather", number, base + 2 + c, at(z + c_off, y, i, f), not_first)

        copy(src, c_dst.at[c], "gather", base + 2, base + 2 + c, mate, first)
        copy(src, z_dst.at[y], "gather", base + 4, base + 4, across, first)

        @pl.when(first)
        def _():
            c_dst[c] = src[...]
            z_dst[y] = src[...]

    def spread_in(c_dst, r_dst, z_dst, base):
        for i in range(2):
            arrived(r_dst.at[i], "gather", base + i)

        @pl.when(not_first)
        def _():
            for i in range(2):
                arrived(c_dst.at[i], "gather", base + 2 + i)

        @pl.when(first)
        def _():
            arrived(c_dst.at[1 - c], "gather", base + 2 + 1 - c)
            arrived(z_dst.at[1 - y], "gather", base + 4)

    travel(0)
    travel(1)
    columns_in(0)
    rows_in(0)
    make_tile(0)
    travel(2)
    rows_in(1)
    make_tile(1)
    columns_in(1)
    make_tile(2)
    travel(3)
    sum_x(0)
    rows_in(2)
    make_tile(3)
    columns_in(2)
    make_tile(4)
    travel(4, range(HALVES // 2))
    sum_x(1)
    sum_x(2)
    rows_in(3)
    make_tile(5)
    columns_in(3)
    make_tile(6)
    travel(4, range(HALVES // 2, HALVES))
    sum_x(3)
    sum_x(4)
    columns_in(4)
    make_tile(7)
    rows_in(4)
    make_tile(8)
    spread_out(width_src, width_c, width_r, width_0, 0)
    sum_x(5)
    sum_x(6)
    spread_in(width_c, width_r, width_0, 0)
    sum_x(7)
    sum_x(8)

    def kernel_blocks(kind, c_width, r_width, dst):
        row = lax.broadcasted_iota(jnp.int32, (PAD, PAD), 0)
        column = lax.broadcasted_iota(jnp.int32, (PAD, PAD), 1)
        inside = (row < ROWS) & (column < ROWS)
        total = keep[kind] + yrecv[kind].astype(F32)
        for j in range(2):
            c_column = column_of(c_width[j, :1, :])
            for i in range(2):
                b = j * 2 + i
                distance = total[:, b * PAD : (b + 1) * PAD]
                exponent = -(distance / (c_column * r_width[i, :1, :])) / FEATURES
                dst[b] = jnp.where(inside, jnp.exp(exponent), 0.0).astype(BF16)

    @pl.when(first)
    def _():
        arrived(yrecv.at[1], "y", 1)
        kernel_blocks(1, width_c, width_0, k0)

    arrived(yrecv.at[0], "y", 0)
    kernel_blocks(0, width_c, width_r, kq)

    def parts_out(index, height, w_of, r_src, c_src, got_r, got_c):
        base = index * 4
        kind = got_r.dtype
        for i in range(2):
            part = dot_nn(w_of("c", 0), kq[i]) + dot_nn(w_of("c", 1), kq[2 + i])
            r_src[i] = part[:height].astype(kind)
            copy(r_src.at[i], got_r.at[y], "parts", base + i, base + y, at(z + r_off, i, c, f))
        for j in range(2):
            part = dot_nt(w_of("r", 0), kq[2 * j]) + dot_nt(w_of("r", 1), kq[2 * j + 1])

            @pl.when(not_first)
            def _(part=part, j=j):
                c_src[j] = part[:height].astype(kind)

            @pl.when(first)
            def _(part=part, j=j):
                own = part + dot_nt(w_of("0", 0), k0[2 * j]) + dot_nt(w_of("0", 1), k0[2 * j + 1])
                c_src[j] = own[:height].astype(kind)

            copy(c_src.at[j], got_c.at[c], "parts", base + 2 + j, base + 2 + c, at(z - c_off, y, j, f), has_c)
        copy(c_src.at[1 - c], got_c.at[c], "parts", base + 2, base + 2 + c, mate, first)

        @pl.when(first)
        def _():
            got_c[c] = c_src[c]

        @pl.when(f == NF - 1)
        def _():
            got_c[...] = jnp.zeros_like(got_c)

    def parts_in(index, got_r, got_c):
        base = index * 4
        for i in range(2):
            arrived(got_r.at[i], "parts", base + i)

        @pl.when(has_c)
        def _():
            for i in range(2):
                arrived(got_c.at[i], "parts", base + 2 + i)

        pl.when(first)(lambda: arrived(got_c.at[1 - c], "parts", base + 2 + 1 - c))
        total = got_r[0].astype(F32) + got_r[1].astype(F32)
        return total + got_c[0].astype(F32) + got_c[1].astype(F32)

    def feat_out(total, got_f, name, base):
        got_f[f] = total.astype(got_f.dtype)
        for i in range(1, NF):
            copy(got_f.at[f], got_f.at[f], name, base + i, base + i, at(z, y, c, (f + i) % NF))

    def feat_in(got_f, name, base):
        for i in range(1, NF):
            arrived(got_f.at[(f + NF - i) % NF], name, base + i)
        total = got_f[0].astype(F32)
        for i in range(1, NF):
            total = total + got_f[i].astype(F32)
        return total

    def gram_q_out(it, mixed):
        gram = dot_nt(mixed, mixed, HIGHEST)
        g_q[it, q] = jnp.concatenate([gram[: NV // 2], gram[NV // 2 :]], axis=1)
        for i in range(1, Q):
            there = (q + i) % Q
            copy(g_q.at[it, q], g_q.at[it, q], "gram_q", 4 * it + i, 4 * it + i, at(z, there // 2, there % 2, f))

    def gram_q_in(it):
        for i in range(1, Q):
            arrived(g_q.at[it, (q + Q - i) % Q], "gram_q", 4 * it + i)
        here = g_q[it, 0]
        for i in range(1, Q):
            here = here + g_q[it, i]
        g_zsrc[it] = here

        @pl.when(first)
        def _():
            g_z[it, 0] = here

        base = 2 * it
        copy(g_zsrc.at[it], g_z.at[it, 0], "gram_z", base, base, at(z - f, y, c, f), not_first)
        copy(g_zsrc.at[it], g_z.at[it, 1], "gram_z", base + 1, base + 1, at(z + 8 - f, y, c, f))

    def gram_z_in(it):
        pl.when(not_first)(lambda: arrived(g_z.at[it, 0], "gram_z", 2 * it))
        arrived(g_z.at[it, 1], "gram_z", 2 * it + 1)
        feat_out(g_z[it, 0] + g_z[it, 1], g_f.at[it], "gram_f", 8 * it)

    def gram_f_in(it):
        pair = feat_in(g_f.at[it], "gram_f", 8 * it) / TOTAL
        return jnp.concatenate([pair[:, :NV], pair[:, NV:]], axis=0)

    ones = jnp.ones((16, PAD), BF16)
    parts_out(0, 8, lambda kind, i: ones, d_rsrc, d_csrc, d_r, d_c)
    feat_out(parts_in(0, d_r, d_c), d_f, "feat", 0)
    degree = feat_in(d_f, "feat", 0)[:1]
    scale = jnp.where(lane < ROWS, 1.0 / jnp.sqrt(jnp.where(lane < ROWS, degree, 1.0)), 0.0)

    def rows_out(it, vectors):
        w_src[it] = (scale * vectors).astype(BF16)
        spread_out(w_src.at[it], w_c.at[it], w_r.at[it], w_0.at[it], 5 * (it + 1))

    def rows_back(it):
        spread_in(w_c.at[it], w_r.at[it], w_0.at[it], 5 * (it + 1))

        def w_of(kind, i):
            return {"c": w_c, "r": w_r, "0": w_0}[kind][it, i]

        parts_out(it + 1, NV, w_of, i_rsrc.at[it], i_csrc.at[it], i_r.at[it], i_c.at[it])

    def sums_out(it):
        feat_out(parts_in(it + 1, i_r.at[it], i_c.at[it]), i_f.at[it], "feat", 8 * (it + 1))

    def image_in(it):
        return feat_in(i_f.at[it], "feat", 8 * (it + 1))

    start = jnp.concatenate([start_ref[...], jnp.zeros((NV, PAD - ROWS), F32)], axis=1)
    rows_out(0, start)
    rows_back(0)
    sums_out(0)
    mixed = 0.5 * (start + scale * image_in(0))
    rows_out(1, mixed)
    gram_q_out(0, mixed)
    gram_q_in(0)
    rows_back(1)
    gram_z_in(0)
    sums_out(1)
    mixed = 0.5 * (mixed + scale * image_in(1))
    gram_q_out(1, mixed)
    first_gram = gram_f_in(0)
    gram_q_in(1)
    first_inverse = inverse_factor(first_gram)
    mixed = dot_nn(first_inverse, mixed, HIGHEST)
    gram_z_in(1)
    second_gram = dot_nn(first_inverse, dot_nt(gram_f_in(1), first_inverse, HIGHEST), HIGHEST)
    second_inverse = inverse_factor(second_gram)
    out_ref[...] = dot_nn(second_inverse, mixed, HIGHEST)[:, :ROWS]
    for made, when in pending:
        if when is None:
            made.wait_send()
        else:
            pl.when(when)(made.wait_send)


def per_device(snapshots, spread, start_vectors):
    half_depth = snapshots.shape[1] // HALVES
    vmem = pltpu.VMEM
    shapes = [
        vmem((HOPS + 1, 2, HALVES, PAD, half_depth), BF16),
        vmem((HOPS + 1, 2, HALVES, PAD, half_depth), BF16),
        vmem((9, PAD, WIDE), BF16),
        vmem((3, 3, PAD, WIDE), BF16),
        vmem((2, PAD, WIDE), BF16),
        vmem((2, PAD, WIDE), BF16),
        vmem((2, PAD, WIDE), F32),
        vmem((4, PAD, PAD), BF16),
        vmem((4, PAD, PAD), BF16),
        vmem((8, PAD), F32),
        vmem((2, 8, PAD), F32),
        vmem((2, 8, PAD), F32),
        vmem((2, 8, PAD), F32),
        vmem((2, NV, PAD), BF16),
        vmem((2, 2, NV, PAD), BF16),
        vmem((2, 2, NV, PAD), BF16),
        vmem((2, 2, NV, PAD), BF16),
        vmem((2, 8, PAD), F32),
        vmem((2, 8, PAD), F32),
        vmem((2, 8, PAD), F32),
        vmem((2, 8, PAD), F32),
        vmem((NF, 8, PAD), F32),
        vmem((2, 2, NV, PAD), BF16),
        vmem((2, 2, NV, PAD), BF16),
        vmem((2, 2, NV, PAD), BF16),
        vmem((2, 2, NV, PAD), BF16),
        vmem((2, NF, NV, PAD), BF16),
        vmem((2, Q, NV // 2, 2 * NV), F32),
        vmem((2, NV // 2, 2 * NV), F32),
        vmem((2, 2, NV // 2, 2 * NV), F32),
        vmem((2, NF, NV // 2, 2 * NV), F32),
        pltpu.SemaphoreType.DMA((N_IDS,)),
        pltpu.SemaphoreType.DMA((N_IDS,)),
    ]
    basis = pl.pallas_call(
        kernel,
        out_shape=jax.ShapeDtypeStruct(start_vectors.shape[::-1], F32),
        in_specs=[pl.BlockSpec(memory_space=pltpu.VMEM)] * 3,
        out_specs=pl.BlockSpec(memory_space=pltpu.VMEM),
        scratch_shapes=shapes,
        compiler_params=pltpu.CompilerParams(
            collective_id=0, has_side_effects=True, vmem_limit_bytes=40 * 1024 * 1024
        ),
        cost_estimate=pl.CostEstimate(
            flops=4_000_000_000, bytes_accessed=400_000, transcendentals=200_000
        ),
        name="subspace",
    )(snapshots, spread.reshape(1, -1), start_vectors.T)
    return basis.T


def solution(mesh):
    return jax.shard_map(
        per_device,
        mesh=mesh,
        in_specs=(P("snap", "feat"), P("snap"), P("snap", None)),
        out_specs=P("snap", None),
        check_vma=False,
    )
```

time: 218 us -> 146 us (0.67)
  Pallas kernels: 213 us -> 142 us
    pallas_call x1, Pallas kernels: 213 us -> 142 us  [per_device(): pl.pallas_call(kernel, out_shape=jax.ShapeDtypeStruct(start_vectors.shape...]
where the time goes in v2:
time: 146 us; the launch traced here: 145 us
  Pallas kernels  142 us (97%)
  local copies, waits for them, and re-layouts  3.1 us (2%)
    pallas_call x1, Pallas kernels, per_device(): pl.pallas_call(kernel, out_shape=jax.ShapeDtypeStruct(start_vectors.shape...  142 us
    unnamed x7, local copies, waits for them, and re-layouts  3.09 us

profile of v2, /device:TPU:1, one launch (start us, length us, event | category | flops | bytes accessed | tf_op | source)
XLA Modules:
  0.0 145.2 jit_solution(6617759193509864110)
XLA Ops:
  0.0 0.0 copy-start.2
  0.0 0.7 copy-done.2
  0.7 0.0 copy-start
  0.7 1.0 copy-done
  1.6 0.0 copy-start.1
  1.6 0.8 copy-done.1
  2.5 142.1 %subspace.1 = f32[64,152]{1,0:T(8,128)S(1)} custom-call(bf16[152,1024]{1,0:T(8,128)(2,1)S(1)} %copy-done, bf16[1,152]{1,0:T(2,128)(2,1)S(1)} %reshape.3.spread_ref, f32[64,152]{1,0:T(8,128)S(1)} %bitcast.3), custom_call_target="tpu_custom_call" | custom-call | flops 4000000000 | bytes 400000 | tf_op jit(solution)/shard_map/subspace/pallas_call | solution.py:566
  144.6 0.6 copy.5
  (1 shorter events, 0.0 us)
Async XLA Ops:
  0.0 0.7 copy-start.2
  0.7 1.0 copy-start
  1.6 0.8 copy-start.1

commit v3 on v2

--- a/solution.py
+++ b/solution.py
@@ -14,6 +14,7 @@
 ROWS = 152
 PAD = 160
 WIDE = 4 * PAD
+NARROW = 384
 NV = 64
 FEATURES = 8192
 TOTAL = Z * Q * ROWS
@@ -52,14 +53,29 @@
 
 def inverse_factor(gram):
     n = gram.shape[0]
-    both = jnp.concatenate([gram, eye(n).astype(F32)], axis=1)
-    rows = lax.broadcasted_iota(jnp.int32, (n, 1), 0)
-    for j in range(n - 1):
-        pivot_row = both[j : j + 1, :]
-        factor = both[:, j : j + 1] * (1.0 / pivot_row[:, j : j + 1])
-        both = both - jnp.where(rows > j, factor, 0.0) * pivot_row
+    on_diagonal = jnp.where(eye(n), gram, 0.0)
+    scale_column = lax.rsqrt(jnp.sum(on_diagonal, axis=1, keepdims=True))
+    scale_row = lax.rsqrt(jnp.sum(on_diagonal, axis=0, keepdims=True))
+    both = jnp.concatenate([gram * scale_column * scale_row, eye(n).astype(F32)], axis=1)
+    groups = [both[8 * g : 8 * g + 8] for g in range(n // 8)]
+    rows = lax.broadcasted_iota(jnp.int32, (8, 2 * n), 0)
+    for j in range(0, n, 2):
+        top, r = j // 8, j % 8
+        left = {g: jnp.broadcast_to(groups[g][:, j : j + 1], (8, 2 * n)) for g in range(top, n // 8)}
+        right = {g: jnp.broadcast_to(groups[g][:, j + 1 : j + 2], (8, 2 * n)) for g in range(top, n // 8)}
+        row0, row1 = groups[top][r : r + 1, :], groups[top][r + 1 : r + 2, :]
+        a, b, d = left[top][r : r + 1, :], left[top][r + 1 : r + 2, :], right[top][r + 1 : r + 2, :]
+        over = 1.0 / (a * d - b * b)
+        add0, add1 = (d * row0 - b * row1) * over, (a * row1 - b * row0) * over
+        step = b * (1.0 / a) * row0
+        for g in range(top, n // 8):
+            change = left[g] * add0 + right[g] * add1
+            if g == top:
+                change = jnp.where(rows > r + 1, change, jnp.where(rows == r + 1, step, 0.0))
+            groups[g] = groups[g] - change
+    both = jnp.concatenate(groups, axis=0)
     diagonal = jnp.sum(jnp.where(eye(n), both[:, :n], 0.0), axis=1, keepdims=True)
-    return both[:, n:] * lax.rsqrt(diagonal)
+    return both[:, n:] * lax.rsqrt(diagonal) * scale_row
 
 
 def count_ids():
@@ -140,8 +156,10 @@
     c_off = k // 2 + is_7
     first = f == 0
     not_first = f != 0
-    has_c = not_first & (f != NF - 1)
     half_depth = cbuf.shape[4]
+    upper = z >= Z // 2
+    last_rows = (y + upper.astype(jnp.int32)) % 2
+    member = q * 2 + yh
 
     def at(zz, yy, cc, ff):
         return {"snap": ((zz + Z) % Z) * Q + yy * 2 + cc, "feat": ff}
@@ -205,7 +223,7 @@
             number = (h + 1) * HALVES + half
             copy(src, rbuf.at[h + 1, y, half], "down", number, number, at(z - 1, y, c, f))
         number = h * HALVES + half
-        copy(src, rbuf.at[h, y, half], "across", number, number, across)
+        copy(src, rbuf.at[h, y, half], "across", number, number, across, upper if h == HOPS else None)
 
     def send_up(h, half):
         src = cbuf.at[h, c, half]
@@ -226,32 +244,49 @@
             send_up(h, half)
 
     def norms(ref, h, i):
-        total = jnp.zeros((PAD, 1), F32)
+        total = jnp.zeros((PAD, half_depth), F32)
         for half in range(HALVES):
             wide = ref[h, i, half].astype(F32)
-            total = total + jnp.sum(wide * wide, axis=1, keepdims=True)
-        return total
+            total = total + wide * wide
+        return jnp.sum(total, axis=1, keepdims=True)
+
+    known = {}
+
+    def c_norms(h):
+        if ("c", h) not in known:
+            known["c", h] = [norms(cbuf, h, j) for j in range(2)]
+        return known["c", h]
+
+    def r_norms(h, picks):
+        if ("r", h) not in known:
+            known["r", h] = [row_of(norms(rbuf, h, i)) for i in picks]
+        return known["r", h]
 
     def owner_of(kk):
         return (0, 0, 2) if kk == 0 else ((kk - 1) % NX, (kk - 1) // NX, (kk - 1) // NX)
 
+    def tile(ref, kk, *place):
+        return ref.at[place + (slice(None), slice(0, NARROW if kk == 8 else WIDE))]
+
     def make_tile(kk):
         r, h = R_OFF[kk], C_OFF[kk]
-        c_norms = [norms(cbuf, h, j) for j in range(2)]
-        r_norms = [row_of(norms(rbuf, r, i)) for i in range(2)]
+        picks = [last_rows] if kk == 8 else [0, 1]
+        c_sums, r_sums = c_norms(h), r_norms(r, picks)
         blocks = []
         for j in range(2):
-            for i in range(2):
+            for n, i in enumerate(picks):
                 inner = dot_nt(cbuf[h, j, 0], rbuf[r, i, 0])
                 for half in range(1, HALVES):
                     inner = inner + dot_nt(cbuf[h, j, half], rbuf[r, i, half])
-                blocks.append(c_norms[j] + r_norms[i] - 2.0 * inner)
-        pbuf[kk] = jnp.concatenate(blocks, axis=1).astype(BF16)
+                blocks.append(c_sums[j] + r_sums[n] - 2.0 * inner)
+        if kk == 8:
+            blocks.append(jnp.zeros((PAD, NARROW - 2 * PAD), F32))
+        tile(pbuf, kk, kk)[...] = jnp.concatenate(blocks, axis=1).astype(BF16)
         owner, _, slot = owner_of(kk)
         source = (x - owner + NX - 1) % NX % 3
         copy(
-            pbuf.at[kk],
-            xbuf.at[slot, source],
+            tile(pbuf, kk, kk),
+            tile(xbuf, kk, slot, source),
             "x",
             kk,
             slot * 3 + source,
@@ -266,22 +301,22 @@
         @pl.when(x == owner)
         def _():
             for i in range(3):
-                arrived(xbuf.at[slot, i], "x", slot * 3 + i)
-            total = pbuf[kk].astype(F32)
+                arrived(tile(xbuf, kk, slot, i), "x", slot * 3 + i)
+            total = tile(pbuf, kk, kk)[...].astype(F32)
             for i in range(3):
-                total = total + xbuf[slot, i].astype(F32)
+                total = total + tile(xbuf, kk, slot, i)[...].astype(F32)
 
             @pl.when(yh == last)
             def _():
-                keep[kind] = total
+                tile(keep, kk, kind)[...] = total
 
             @pl.when(yh != last)
             def _():
-                ysend[kind] = total.astype(BF16)
+                tile(ysend, kk, kind)[...] = total.astype(BF16)
 
         copy(
-            ysend.at[kind],
-            yrecv.at[kind],
+            tile(ysend, kk, kind),
+            tile(yrecv, kk, kind),
             "y",
             kind,
             kind,
@@ -354,7 +389,7 @@
     sum_x(4)
     columns_in(4)
     make_tile(7)
-    rows_in(4)
+    pl.when(upper)(lambda: rows_in(4))
     make_tile(8)
     spread_out(width_src, width_c, width_r, width_0, 0)
     sum_x(5)
@@ -363,26 +398,35 @@
     sum_x(7)
     sum_x(8)
 
-    def kernel_blocks(kind, c_width, r_width, dst):
+    def kernel_block(kind, b, c_column, r_row, dst, place):
         row = lax.broadcasted_iota(jnp.int32, (PAD, PAD), 0)
         column = lax.broadcasted_iota(jnp.int32, (PAD, PAD), 1)
         inside = (row < ROWS) & (column < ROWS)
-        total = keep[kind] + yrecv[kind].astype(F32)
-        for j in range(2):
-            c_column = column_of(c_width[j, :1, :])
-            for i in range(2):
-                b = j * 2 + i
-                distance = total[:, b * PAD : (b + 1) * PAD]
-                exponent = -(distance / (c_column * r_width[i, :1, :])) / FEATURES
-                dst[b] = jnp.where(inside, jnp.exp(exponent), 0.0).astype(BF16)
+        lanes = slice(b * PAD, (b + 1) * PAD)
+        distance = keep[kind, :, lanes] + yrecv[kind, :, lanes].astype(F32)
+        exponent = -(distance / (c_column * r_row)) / FEATURES
+        dst[place] = jnp.where(inside, jnp.exp(exponent), 0.0).astype(BF16)
+
+    c_columns = [column_of(width_c[j, :1, :]) for j in range(2)]
 
     @pl.when(first)
     def _():
         arrived(yrecv.at[1], "y", 1)
-        kernel_blocks(1, width_c, width_0, k0)
-
-    arrived(yrecv.at[0], "y", 0)
-    kernel_blocks(0, width_c, width_r, kq)
+        for b in range(4):
+            kernel_block(1, b, c_columns[b // 2], width_0[b % 2, :1, :], k0, b)
+
+    @pl.when(f != NF - 1)
+    def _():
+        arrived(yrecv.at[0], "y", 0)
+        for b in range(4):
+            kernel_block(0, b, c_columns[b // 2], width_r[b % 2, :1, :], kq, b)
+
+    @pl.when(f == NF - 1)
+    def _():
+        arrived(tile(yrecv, 8, 0), "y", 0)
+        for j in range(2):
+            kq[2 * j + 1 - last_rows] = jnp.zeros((PAD, PAD), BF16)
+            kernel_block(0, j, c_columns[j], width_r[last_rows, :1, :], kq, 2 * j + last_rows)
 
     def parts_out(index, height, w_of, r_src, c_src, got_r, got_c):
         base = index * 4
@@ -403,23 +447,19 @@
                 own = part + dot_nt(w_of("0", 0), k0[2 * j]) + dot_nt(w_of("0", 1), k0[2 * j + 1])
                 c_src[j] = own[:height].astype(kind)
 
-            copy(c_src.at[j], got_c.at[c], "parts", base + 2 + j, base + 2 + c, at(z - c_off, y, j, f), has_c)
+            copy(c_src.at[j], got_c.at[c], "parts", base + 2 + j, base + 2 + c, at(z - c_off, y, j, f), not_first)
         copy(c_src.at[1 - c], got_c.at[c], "parts", base + 2, base + 2 + c, mate, first)
 
         @pl.when(first)
         def _():
             got_c[c] = c_src[c]
-
-        @pl.when(f == NF - 1)
-        def _():
-            got_c[...] = jnp.zeros_like(got_c)
 
     def parts_in(index, got_r, got_c):
         base = index * 4
         for i in range(2):
             arrived(got_r.at[i], "parts", base + i)
 
-        @pl.when(has_c)
+        @pl.when(not_first)
         def _():
             for i in range(2):
                 arrived(got_c.at[i], "parts", base + 2 + i)
@@ -456,21 +496,33 @@
             here = here + g_q[it, i]
         g_zsrc[it] = here
 
-        @pl.when(first)
+        @pl.when(member == 0)
         def _():
             g_z[it, 0] = here
 
         base = 2 * it
-        copy(g_zsrc.at[it], g_z.at[it, 0], "gram_z", base, base, at(z - f, y, c, f), not_first)
-        copy(g_zsrc.at[it], g_z.at[it, 1], "gram_z", base + 1, base + 1, at(z + 8 - f, y, c, f))
+        there = at(z - member, y, c, f)
+        copy(g_zsrc.at[it], g_z.at[it, 0], "gram_z", base, base, there, member != 0)
+        there = at(z + 8 - member, y, c, f)
+        copy(g_zsrc.at[it], g_z.at[it, 1], "gram_z", base + 1, base + 1, there)
 
     def gram_z_in(it):
-        pl.when(not_first)(lambda: arrived(g_z.at[it, 0], "gram_z", 2 * it))
+        pl.when(member != 0)(lambda: arrived(g_z.at[it, 0], "gram_z", 2 * it))
         arrived(g_z.at[it, 1], "gram_z", 2 * it + 1)
-        feat_out(g_z[it, 0] + g_z[it, 1], g_f.at[it], "gram_f", 8 * it)
+        g_f[it, member] = g_z[it, 0] + g_z[it, 1]
+        mine = g_f.at[it, member]
+        for i in range(1, 8):
+            there = (member + i) % 8
+            device = at(z, there // 4, there // 2 % 2, there % 2 * NX + x)
+            copy(mine, mine, "gram_f", 8 * it + i, 8 * it + i, device)
 
     def gram_f_in(it):
-        pair = feat_in(g_f.at[it], "gram_f", 8 * it) / TOTAL
+        for i in range(1, 8):
+            arrived(g_f.at[it, (member + 8 - i) % 8], "gram_f", 8 * it + i)
+        pair = g_f[it, 0]
+        for i in range(1, 8):
+            pair = pair + g_f[it, i]
+        pair = pair / TOTAL
         return jnp.concatenate([pair[:, :NV], pair[:, NV:]], axis=0)
 
     ones = jnp.ones((16, PAD), BF16)
@@ -506,13 +558,12 @@
     gram_q_out(0, mixed)
     gram_q_in(0)
     rows_back(1)
+    sums_out(1)
     gram_z_in(0)
-    sums_out(1)
     mixed = 0.5 * (mixed + scale * image_in(1))
     gram_q_out(1, mixed)
-    first_gram = gram_f_in(0)
     gram_q_in(1)
-    first_inverse = inverse_factor(first_gram)
+    first_inverse = inverse_factor(gram_f_in(0))
     mixed = dot_nn(first_inverse, mixed, HIGHEST)
     gram_z_in(1)
     second_gram = dot_nn(first_inverse, dot_nt(gram_f_in(1), first_inverse, HIGHEST), HIGHEST)

time: 146 us -> 140 us (0.959)
  Pallas kernels: 142 us -> 137 us
    pallas_call x1, Pallas kernels: 142 us -> 137 us  [per_device(): pl.pallas_call(kernel, out_shape=jax.ShapeDtypeStruct(start_vectors.shape...]
where the time goes in v3:
time: 140 us
  Pallas kernels  137 us (98%)
  local copies, waits for them, and re-layouts  3.1 us (2%)
    pallas_call x1, Pallas kernels, per_device(): pl.pallas_call(kernel, out_shape=jax.ShapeDtypeStruct(start_vectors.shape...  137 us
    unnamed x7, local copies, waits for them, and re-layouts  3.09 us

profile of v3, /device:TPU:1, one launch (start us, length us, event | category | flops | bytes accessed | tf_op | source)
XLA Modules:
  0.0 139.7 jit_solution(3029586802379052807)
XLA Ops:
  0.0 0.0 copy-start.2
  0.0 0.7 copy-done.2
  0.7 0.0 copy-start
  0.7 1.0 copy-done
  1.6 0.0 copy-start.1
  1.6 0.8 copy-done.1
  2.5 136.6 %subspace.1 = f32[64,152]{1,0:T(8,128)S(1)} custom-call(bf16[152,1024]{1,0:T(8,128)(2,1)S(1)} %copy-done, bf16[1,152]{1,0:T(2,128)(2,1)S(1)} %reshape.3.spread_ref, f32[64,152]{1,0:T(8,128)S(1)} %bitcast.3), custom_call_target="tpu_custom_call" | custom-call | flops 4000000000 | bytes 400000 | tf_op jit(solution)/shard_map/subspace/pallas_call | solution.py:617
  139.1 0.6 copy.5
  (1 shorter events, 0.0 us)
Async XLA Ops:
  0.0 0.7 copy-start.2
  0.7 1.0 copy-start
  1.6 0.8 copy-start.1

commit v4 on v3

--- a/solution.py
+++ b/solution.py
@@ -150,12 +150,21 @@
     c = q % 2
     x = f % NX
     yh = f // NX
-    k = f + 1
-    is_7 = (k == 7).astype(jnp.int32)
-    r_off = (k + 1) // 2 - is_7
-    c_off = k // 2 + is_7
-    first = f == 0
-    not_first = f != 0
+
+    def tile_of(core):
+        k = f + 1 if core == 0 else NF - f
+        is_7 = (k == 7).astype(jnp.int32)
+        return k, (k + 1) // 2 - is_7, k // 2 + is_7
+
+    (k_a, r_off_a, c_off_a), (k_b, r_off_b, c_off_b) = tile_of(0), tile_of(1)
+    c_offs = [c_off_a, c_off_b]
+    k = k_a + c * (k_b - k_a)
+    r_off = r_off_a + c * (r_off_b - r_off_a)
+    c_off = c_off_a + c * (c_off_b - c_off_a)
+    first = k == 1
+    not_first = k != 1
+    is_last = k == NF
+    from_away = [not_first | (c != i) for i in range(2)]
     half_depth = cbuf.shape[4]
     upper = z >= Z // 2
     last_rows = (y + upper.astype(jnp.int32)) % 2
@@ -263,7 +272,9 @@
         return known["r", h]
 
     def owner_of(kk):
-        return (0, 0, 2) if kk == 0 else ((kk - 1) % NX, (kk - 1) // NX, (kk - 1) // NX)
+        place, last = (0, 0) if kk == 0 else ((kk - 1) % NX, (kk - 1) // NX)
+        owner = place + c * (NX - 1 - 2 * place)
+        return owner, last + c * (1 - 2 * last), 2 if kk == 0 else last
 
     def tile(ref, kk, *place):
         return ref.at[place + (slice(None), slice(0, NARROW if kk == 8 else WIDE))]
@@ -336,10 +347,8 @@
         for i in range(2):
             copy(src, r_dst.at[y], "gather", base + i, base + y, at(z - r_off, i, c, f))
         for i in range(2):
-            number = base + 2 + i
-            copy(src, c_dst.at[c], "gather", number, base + 2 + c, at(z + c_off, y, i, f), not_first)
-
-        copy(src, c_dst.at[c], "gather", base + 2, base + 2 + c, mate, first)
+            there = at(z + c_offs[i], y, i, f)
+            copy(src, c_dst.at[c], "gather", base + 2 + i, base + 2 + c, there, from_away[i])
         copy(src, z_dst.at[y], "gather", base + 4, base + 4, across, first)
 
         @pl.when(first)
@@ -350,16 +359,9 @@
     def spread_in(c_dst, r_dst, z_dst, base):
         for i in range(2):
             arrived(r_dst.at[i], "gather", base + i)
-
-        @pl.when(not_first)
-        def _():
-            for i in range(2):
-                arrived(c_dst.at[i], "gather", base + 2 + i)
-
-        @pl.when(first)
-        def _():
-            arrived(c_dst.at[1 - c], "gather", base + 2 + 1 - c)
-            arrived(z_dst.at[1 - y], "gather", base + 4)
+        for i in range(2):
+            pl.when(from_away[i])(lambda i=i: arrived(c_dst.at[i], "gather", base + 2 + i))
+        pl.when(first)(lambda: arrived(z_dst.at[1 - y], "gather", base + 4))
 
     travel(0)
     travel(1)
@@ -415,13 +417,13 @@
         for b in range(4):
             kernel_block(1, b, c_columns[b // 2], width_0[b % 2, :1, :], k0, b)
 
-    @pl.when(f != NF - 1)
+    @pl.when(jnp.logical_not(is_last))
     def _():
         arrived(yrecv.at[0], "y", 0)
         for b in range(4):
             kernel_block(0, b, c_columns[b // 2], width_r[b % 2, :1, :], kq, b)
 
-    @pl.when(f == NF - 1)
+    @pl.when(is_last)
     def _():
         arrived(tile(yrecv, 8, 0), "y", 0)
         for j in range(2):
@@ -447,8 +449,8 @@
                 own = part + dot_nt(w_of("0", 0), k0[2 * j]) + dot_nt(w_of("0", 1), k0[2 * j + 1])
                 c_src[j] = own[:height].astype(kind)
 
-            copy(c_src.at[j], got_c.at[c], "parts", base + 2 + j, base + 2 + c, at(z - c_off, y, j, f), not_first)
-        copy(c_src.at[1 - c], got_c.at[c], "parts", base + 2, base + 2 + c, mate, first)
+            there = at(z - c_off, y, j, f)
+            copy(c_src.at[j], got_c.at[c], "parts", base + 2 + j, base + 2 + c, there, from_away[j])
 
         @pl.when(first)
         def _():
@@ -459,12 +461,8 @@
         for i in range(2):
             arrived(got_r.at[i], "parts", base + i)
 
-        @pl.when(not_first)
-        def _():
-            for i in range(2):
-                arrived(got_c.at[i], "parts", base + 2 + i)
-
-        pl.when(first)(lambda: arrived(got_c.at[1 - c], "parts", base + 2 + 1 - c))
+        for i in range(2):
+            pl.when(from_away[i])(lambda i=i: arrived(got_c.at[i], "parts", base + 2 + i))
         total = got_r[0].astype(F32) + got_r[1].astype(F32)
         return total + got_c[0].astype(F32) + got_c[1].astype(F32)
 

time: 140 us -> 134 us (0.957)
  Pallas kernels: 137 us -> 130 us
    pallas_call x1, Pallas kernels: 137 us -> 130 us  [per_device(): pl.pallas_call(kernel, out_shape=jax.ShapeDtypeStruct(start_vectors.shape...]
where the time goes in v4:
time: 134 us; the launch traced here: 133 us
  Pallas kernels  130 us (97%)
  local copies, waits for them, and re-layouts  3.1 us (2%)
    pallas_call x1, Pallas kernels, per_device(): pl.pallas_call(kernel, out_shape=jax.ShapeDtypeStruct(start_vectors.shape...  130 us
    unnamed x7, local copies, waits for them, and re-layouts  3.09 us

profile of v4, /device:TPU:1, one launch (start us, length us, event | category | flops | bytes accessed | tf_op | source)
XLA Modules:
  0.0 133.1 jit_solution(4333322710550882642)
XLA Ops:
  0.0 0.0 copy-start.2
  0.0 0.7 copy-done.2
  0.7 0.0 copy-start
  0.7 1.0 copy-done
  1.6 0.0 copy-start.1
  1.6 0.8 copy-done.1
  2.5 130.0 %subspace.1 = f32[64,152]{1,0:T(8,128)S(1)} custom-call(bf16[152,1024]{1,0:T(8,128)(2,1)S(1)} %copy-done, bf16[1,152]{1,0:T(2,128)(2,1)S(1)} %reshape.3.spread_ref, f32[64,152]{1,0:T(8,128)S(1)} %bitcast.3), custom_call_target="tpu_custom_call" | custom-call | flops 4000000000 | bytes 400000 | tf_op jit(solution)/shard_map/subspace/pallas_call | solution.py:615
  132.4 0.6 copy.5
  (1 shorter events, 0.0 us)
Async XLA Ops:
  0.0 0.7 copy-start.2
  0.7 1.0 copy-start
  1.6 0.8 copy-start.1

commit v5 on v4

--- a/solution.py
+++ b/solution.py
@@ -23,6 +23,7 @@
 HIGHEST = lax.Precision.HIGHEST
 R_OFF = (0, 1, 1, 2, 2, 3, 3, 3, 4)
 C_OFF = (0, 0, 1, 1, 2, 2, 3, 4, 4)
+FEAT_STEPS = ((2, 1), (1, 1), (3, 1), (0, 1), (2, 0), (1, 0), (3, 0))
 
 
 def dot_nt(a, b, precision=None):
@@ -192,6 +193,17 @@
             pl.when(when)(made.start)
         pending.append((made, when))
 
+    marks = [0, 0]
+
+    def settle(everything=False):
+        until = len(pending) if everything else marks[1]
+        for made, when in pending[marks[0] : until]:
+            if when is None:
+                made.wait_send()
+            else:
+                pl.when(when)(made.wait_send)
+        marks[0], marks[1] = until, len(pending)
+
     def arrived(dst, name, recv):
         pltpu.make_async_remote_copy(
             src_ref=dst,
@@ -215,8 +227,6 @@
         rest = jnp.zeros((PAD - ROWS, half_depth), BF16)
         cbuf[0, c, half, :ROWS, :] = part
         cbuf[0, c, half, ROWS:, :] = rest
-        rbuf[0, y, half, :ROWS, :] = part
-        rbuf[0, y, half, ROWS:, :] = rest
     lane = lax.broadcasted_iota(jnp.int32, (1, PAD), 1)
     width_src[...] = jnp.broadcast_to(
         jnp.concatenate(
@@ -227,7 +237,7 @@
     pl.semaphore_wait(barrier, len(near))
 
     def send_down(h, half):
-        src = rbuf.at[h, y, half]
+        src = rbuf.at[h, y, half] if h > 0 else cbuf.at[0, c, half]
         if h < HOPS:
             number = (h + 1) * HALVES + half
             copy(src, rbuf.at[h + 1, y, half], "down", number, number, at(z - 1, y, c, f))
@@ -364,6 +374,7 @@
         pl.when(first)(lambda: arrived(z_dst.at[1 - y], "gather", base + 4))
 
     travel(0)
+    rbuf[0, y] = cbuf[0, c]
     travel(1)
     columns_in(0)
     rows_in(0)
@@ -380,19 +391,19 @@
     columns_in(2)
     make_tile(4)
     travel(4, range(HALVES // 2))
-    sum_x(1)
-    sum_x(2)
     rows_in(3)
     make_tile(5)
     columns_in(3)
     make_tile(6)
     travel(4, range(HALVES // 2, HALVES))
-    sum_x(3)
-    sum_x(4)
     columns_in(4)
     make_tile(7)
     pl.when(upper)(lambda: rows_in(4))
     make_tile(8)
+    sum_x(1)
+    sum_x(2)
+    sum_x(3)
+    sum_x(4)
     spread_out(width_src, width_c, width_r, width_0, 0)
     sum_x(5)
     sum_x(6)
@@ -468,12 +479,14 @@
 
     def feat_out(total, got_f, name, base):
         got_f[f] = total.astype(got_f.dtype)
-        for i in range(1, NF):
-            copy(got_f.at[f], got_f.at[f], name, base + i, base + i, at(z, y, c, (f + i) % NF))
+        for i, (dx, dy) in enumerate(FEAT_STEPS):
+            there = (yh + dy) % 2 * NX + (x + dx) % NX
+            copy(got_f.at[f], got_f.at[f], name, base + i, base + i, at(z, y, c, there))
 
     def feat_in(got_f, name, base):
-        for i in range(1, NF):
-            arrived(got_f.at[(f + NF - i) % NF], name, base + i)
+        for i, (dx, dy) in enumerate(FEAT_STEPS):
+            source = (yh + dy) % 2 * NX + (x + NX - dx) % NX
+            arrived(got_f.at[source], name, base + i)
         total = got_f[0].astype(F32)
         for i in range(1, NF):
             total = total + got_f[i].astype(F32)
@@ -524,8 +537,11 @@
         return jnp.concatenate([pair[:, :NV], pair[:, NV:]], axis=0)
 
     ones = jnp.ones((16, PAD), BF16)
+    settle()
     parts_out(0, 8, lambda kind, i: ones, d_rsrc, d_csrc, d_r, d_c)
+    settle()
     feat_out(parts_in(0, d_r, d_c), d_f, "feat", 0)
+    settle()
     degree = feat_in(d_f, "feat", 0)[:1]
     scale = jnp.where(lane < ROWS, 1.0 / jnp.sqrt(jnp.where(lane < ROWS, degree, 1.0)), 0.0)
 
@@ -549,29 +565,33 @@
 
     start = jnp.concatenate([start_ref[...], jnp.zeros((NV, PAD - ROWS), F32)], axis=1)
     rows_out(0, start)
+    settle()
     rows_back(0)
     sums_out(0)
+    settle()
     mixed = 0.5 * (start + scale * image_in(0))
     rows_out(1, mixed)
     gram_q_out(0, mixed)
+    settle()
     gram_q_in(0)
     rows_back(1)
     sums_out(1)
+    settle()
     gram_z_in(0)
     mixed = 0.5 * (mixed + scale * image_in(1))
     gram_q_out(1, mixed)
+    settle()
     gram_q_in(1)
+    settle()
     first_inverse = inverse_factor(gram_f_in(0))
     mixed = dot_nn(first_inverse, mixed, HIGHEST)
     gram_z_in(1)
+    settle()
+    settle()
     second_gram = dot_nn(first_inverse, dot_nt(gram_f_in(1), first_inverse, HIGHEST), HIGHEST)
     second_inverse = inverse_factor(second_gram)
     out_ref[...] = dot_nn(second_inverse, mixed, HIGHEST)[:, :ROWS]
-    for made, when in pending:
-        if when is None:
-            made.wait_send()
-        else:
-            pl.when(when)(made.wait_send)
+    settle(everything=True)
 
 
 def per_device(snapshots, spread, start_vectors):

time: 134 us -> 131 us (0.978)
  Pallas kernels: 130 us -> 128 us
    pallas_call x1, Pallas kernels: 130 us -> 128 us  [per_device(): pl.pallas_call(kernel, out_shape=jax.ShapeDtypeStruct(start_vectors.shape...]
where the time goes in v5:
time: 131 us
  Pallas kernels  128 us (98%)
  local copies, waits for them, and re-layouts  3.1 us (2%)
    pallas_call x1, Pallas kernels, per_device(): pl.pallas_call(kernel, out_shape=jax.ShapeDtypeStruct(start_vectors.shape...  128 us
    unnamed x7, local copies, waits for them, and re-layouts  3.09 us

profile of v5, /device:TPU:1, one launch (start us, length us, event | category | flops | bytes accessed | tf_op | source)
XLA Modules:
  0.0 131.2 jit_solution(14270238306021217098)
XLA Ops:
  0.0 0.0 copy-start.2
  0.0 0.7 copy-done.2
  0.7 0.0 copy-start
  0.7 1.0 copy-done
  1.6 0.0 copy-start.1
  1.6 0.8 copy-done.1
  2.5 128.1 %subspace.1 = f32[64,152]{1,0:T(8,128)S(1)} custom-call(bf16[152,1024]{1,0:T(8,128)(2,1)S(1)} %copy-done, bf16[1,152]{1,0:T(2,128)(2,1)S(1)} %reshape.3.spread_ref, f32[64,152]{1,0:T(8,128)S(1)} %bitcast.3), custom_call_target="tpu_custom_call" | custom-call | flops 4000000000 | bytes 400000 | tf_op jit(solution)/shard_map/subspace/pallas_call | solution.py:635
  130.6 0.6 copy.5
  (1 shorter events, 0.0 us)
Async XLA Ops:
  0.0 0.7 copy-start.2
  0.7 1.0 copy-start
  1.6 0.8 copy-start.1

commit v6 on v5

--- a/solution.py
+++ b/solution.py
@@ -411,35 +411,41 @@
     sum_x(7)
     sum_x(8)
 
-    def kernel_block(kind, b, c_column, r_row, dst, place):
+    def rate(c_column, r_row):
+        return -1.0 / (c_column * r_row * FEATURES)
+
+    def kernel_block(kind, b, factor, dst, place):
         row = lax.broadcasted_iota(jnp.int32, (PAD, PAD), 0)
         column = lax.broadcasted_iota(jnp.int32, (PAD, PAD), 1)
         inside = (row < ROWS) & (column < ROWS)
         lanes = slice(b * PAD, (b + 1) * PAD)
         distance = keep[kind, :, lanes] + yrecv[kind, :, lanes].astype(F32)
-        exponent = -(distance / (c_column * r_row)) / FEATURES
-        dst[place] = jnp.where(inside, jnp.exp(exponent), 0.0).astype(BF16)
+        dst[place] = jnp.where(inside, jnp.exp(distance * factor), 0.0).astype(BF16)
 
     c_columns = [column_of(width_c[j, :1, :]) for j in range(2)]
 
     @pl.when(first)
     def _():
+        factors = [rate(c_columns[b // 2], width_0[b % 2, :1, :]) for b in range(4)]
         arrived(yrecv.at[1], "y", 1)
         for b in range(4):
-            kernel_block(1, b, c_columns[b // 2], width_0[b % 2, :1, :], k0, b)
+            kernel_block(1, b, factors[b], k0, b)
 
     @pl.when(jnp.logical_not(is_last))
     def _():
+        factors = [rate(c_columns[b // 2], width_r[b % 2, :1, :]) for b in range(4)]
         arrived(yrecv.at[0], "y", 0)
         for b in range(4):
-            kernel_block(0, b, c_columns[b // 2], width_r[b % 2, :1, :], kq, b)
+            kernel_block(0, b, factors[b], kq, b)
 
     @pl.when(is_last)
     def _():
+        factors = [rate(c_columns[j], width_r[last_rows, :1, :]) for j in range(2)]
+        for j in range(2):
+            kq[2 * j + 1 - last_rows] = jnp.zeros((PAD, PAD), BF16)
         arrived(tile(yrecv, 8, 0), "y", 0)
         for j in range(2):
-            kq[2 * j + 1 - last_rows] = jnp.zeros((PAD, PAD), BF16)
-            kernel_block(0, j, c_columns[j], width_r[last_rows, :1, :], kq, 2 * j + last_rows)
+            kernel_block(0, j, factors[j], kq, 2 * j + last_rows)
 
     def parts_out(index, height, w_of, r_src, c_src, got_r, got_c):
         base = index * 4

time: 131 us -> 132 us (level)
  no operation moved by 1% of the time
where the time goes in v6:
time: 132 us
  Pallas kernels  129 us (98%)
  local copies, waits for them, and re-layouts  3.1 us (2%)
    pallas_call x1, Pallas kernels, per_device(): pl.pallas_call(kernel, out_shape=jax.ShapeDtypeStruct(start_vectors.shape...  129 us
    unnamed x7, local copies, waits for them, and re-layouts  3.09 us

profile of v6, /device:TPU:1, one launch (start us, length us, event | category | flops | bytes accessed | tf_op | source)
XLA Modules:
  0.0 132.0 jit_solution(11410085702162608658)
XLA Ops:
  0.0 0.0 copy-start.2
  0.0 0.7 copy-done.2
  0.7 0.0 copy-start
  0.7 1.0 copy-done
  1.6 0.0 copy-start.1
  1.6 0.8 copy-done.1
  2.5 128.9 %subspace.1 = f32[64,152]{1,0:T(8,128)S(1)} custom-call(bf16[152,1024]{1,0:T(8,128)(2,1)S(1)} %copy-done, bf16[1,152]{1,0:T(2,128)(2,1)S(1)} %reshape.3.spread_ref, f32[64,152]{1,0:T(8,128)S(1)} %bitcast.3), custom_call_target="tpu_custom_call" | custom-call | flops 4000000000 | bytes 400000 | tf_op jit(solution)/shard_map/subspace/pallas_call | solution.py:641
  131.3 0.6 copy.5
  (1 shorter events, 0.0 us)
Async XLA Ops:
  0.0 0.7 copy-start.2
  0.7 1.0 copy-start
  1.6 0.8 copy-start.1
